TPU v7x, 512 devices: a whole 4x8x8 slice. The times are simulated.
512 devices in a mesh: blk: 64 (over y, x, z_lo), freq: 8 (over z_hi, core).
Axes of the slice: x: 4, y: 8, z: 8 (z_hi: 4, z_lo: 2; z = z_hi * 2 + z_lo), core: 2. Of those that a mesh axis runs over, the one named last changes fastest.
Arguments:
- recorded: bfloat16 [8, 2, 1024, 16384], P('freq', None, 'blk'), may hold values from -6 to 6
- mirror: bfloat16 [8, 2, 192, 16384], P('freq', None, None, 'blk')
- live_counts: int32 [8, 64], P('freq', 'blk'), may hold values from 64 to 256, as said below
- bins: int32 [8, 1024, 2], P('freq', 'blk'), may hold values from 0 to 127, as said below
- bin_weight: float32 [8, 1024, 2], P('freq', 'blk'), may hold values from 0.25 to 1
- taper_lo: int32 [8, 1024], P('freq', 'blk'), may hold values from 0 to 47
- taper_hi: int32 [8, 1024], P('freq', 'blk'), may hold values from 144 to 192
- gain: float32 [8], P('freq'), as said below
Outputs:
- predicted: float32 [8, 2, 128, 192], P('freq', None, 'blk')
Inputs may be any that keep to these rules, and one draw needn't show every extreme that they name: `live_counts`: in each frequency slice one block is fully live. The two bins of a trace differ. Among the 32 entries of the traces of one device, no bin is named more than 2 times; one bin is named exactly 2 times by the traces of every device. `gain`: Positive.
All inputs are finite; a program needn't handle non-finite values.
Results may differ from a plain program's by a relative error of at most 0.0003.
Values may be sent and summed in bfloat16 or wider, within the bound.
A program may use at most 64 MiB of HBM per device.

v0:
```python
import jax
import jax.numpy as jnp
from jax import lax
from jax.sharding import PartitionSpec as P

MOST = 2
RAMP = 24


def taper_weights(lo_col, hi_col, count):
    column = jnp.arange(count, dtype=jnp.int32).astype(jnp.float32)[None, None, :]
    rise = jnp.clip((column - lo_col.astype(jnp.float32)[:, :, None] + 1.0) / RAMP, 0.0, 1.0)
    fall = jnp.clip((hi_col.astype(jnp.float32)[:, :, None] - column) / RAMP, 0.0, 1.0)
    return rise * fall


def combine_parts(prod):
    real_part = prod[:, 0, :, 0] - prod[:, 1, :, 1]
    imag_part = prod[:, 0, :, 1] + prod[:, 1, :, 0]
    return (real_part, imag_part)


def local(recorded, mirror, live_counts, bins, bin_weight, taper_lo, taper_hi, gain):
    f_dev, _, r_dev, surf = recorded.shape
    src = mirror.shape[2]
    surf_dev = mirror.shape[3]
    n_blk = lax.axis_size("blk")
    bins_dev = max(2, (2 * r_dev + n_blk - 1) // n_blk)
    total_bins = bins_dev * n_blk
    offset = jnp.arange(surf_dev, dtype=jnp.int32)
    live = offset[None, :] < live_counts
    masked = jnp.where(live[:, None, None, :], mirror, jnp.zeros_like(mirror))
    prod = jnp.einsum(
        "fark,fbsk->farbs",
        recorded,
        lax.all_gather(masked, "blk", axis=3, tiled=True),
        preferred_element_type=jnp.float32,
    )
    real_part, imag_part = combine_parts(prod)
    taper = taper_weights(taper_lo, taper_hi, src)
    values = jnp.stack([real_part * taper, imag_part * taper], axis=2)
    flat_bins = bins.reshape(f_dev, 2 * r_dev)
    flat_weight = bin_weight.reshape(f_dev, 2 * r_dev)
    onehot = (
        flat_bins[:, :, None] == jnp.arange(total_bins, dtype=jnp.int32)[None, None, :]
    ).astype(jnp.int32)
    rank = jnp.sum(jnp.cumsum(onehot, axis=1) * onehot, axis=2) - 1
    slot_id = flat_bins * MOST + rank
    slot_ids = jnp.arange(total_bins * MOST, dtype=jnp.int32)
    select = jnp.where(slot_id[:, None, :] == slot_ids[None, :, None], flat_weight[:, None, :], 0.0)
    entry_values = jnp.repeat(values.reshape(f_dev, r_dev, 2 * src), 2, axis=1)
    outgoing = jnp.einsum("fle,fec->flc", select, entry_values, precision=lax.Precision.HIGHEST)
    outgoing = outgoing.reshape(f_dev, n_blk, bins_dev * MOST, 2 * src)
    incoming = lax.all_to_all(outgoing, "blk", split_axis=1, concat_axis=1, tiled=True)
    summed = incoming.reshape(f_dev, n_blk, bins_dev, MOST, 2, src).sum(axis=(1, 3))
    binned = jnp.transpose(summed, (0, 2, 1, 3))
    scaled = binned * gain[:, None, None, None]
    local_energy = jnp.sum(scaled * scaled, axis=(0, 1, 3))
    total_energy = lax.psum(local_energy, "freq")
    slices = f_dev * lax.axis_size("freq")
    norm = jnp.sqrt(total_energy / (slices * 2 * src) + 1e-06)
    return scaled / norm[None, None, :, None]


def solution(mesh):
    in_specs = (
        P("freq", None, "blk", None),
        P("freq", None, None, "blk"),
        P("freq", "blk"),
        P("freq", "blk", None),
        P("freq", "blk", None),
        P("freq", "blk"),
        P("freq", "blk"),
        P("freq"),
    )
    out_specs = P("freq", None, "blk", None)
    return jax.shard_map(local, mesh=mesh, in_specs=in_specs, out_specs=out_specs, check_vma=False)
```

profile of v0, /device:TPU:1, one launch (start us, length us, event | category | flops | bytes accessed | tf_op | source)
XLA Modules:
  0.0 427.0 jit_solution(13802961099593379704)
XLA Ops:
  7.3 1.6 broadcast_select_fusion
  8.9 0.0 all-gather.2.cloned.1.call-update
  9.0 0.8 copy.25
  9.7 0.1 broadcast_in_dim.40
  9.8 0.8 copy.24
  10.6 0.1 reshape.498
  10.6 0.1 fusion.17
  10.7 0.1 reduce_window_sum.11
  10.8 0.2 select_reduce_fusion
  11.0 0.7 convert_bitcast_fusion
  11.7 323.4 %all-gather.2.cloned.1.call-done = bf16[1,2,192,16384]{3,2,1,0:T(8,128)(2,1)} async-done(((bf16[1,2,192,256]{3,2,1,0:T(8,128)(2,1)}), bf16[1,2,192,16384]{3,2,1,0:T(8,128)(2,1)}) %all-gather.2.cloned.1.call-update) | async-done | bytes 12582928 | tf_op jit(solution)/shard_map/all_gather | solution.py:36
  335.1 8.5 %fusion.2 = f32[1,2,16,2,192]{4,2,1,3,0:T(8,128)S(1)} fusion(bf16[1,2,192,16384]{3,2,1,0:T(8,128)(2,1)} %all-gather.2.cloned.1.call-done, bf16[1,2,16,16384]{3,2,1,0:T(8,128)(2,1)S(1)} %copy-done), kind=kOutput, calls=%fused_computation.3 | convolution fusion | flops 402653184 | bytes 13680640 | tf_op jit(solution)/shard_map/fark,fbsk->farbs/dot_general | solution.py:33
  343.6 0.1 fusion.16
  343.7 0.1 reshape.501
  343.9 0.6 convolution_bitcast_fusion
  344.5 1.0 copy.29
  345.5 6.6 %all-to-all-start = ((f32[1,64,4,384]{3,2,0,1:T(4,128)}), f32[1,64,4,384]{3,2,0,1:T(4,128)S(1)}, u32[]{:S(2)}, u32[]{:S(2)}) async-start(f32[1,64,4,384]{3,2,0,1:T(4,128)} %copy.29), calls=%async_computation | async-start | bytes 786432 | tf_op jit(solution)/shard_map/all_to_all | solution.py:54
  352.8 10.9 %all-to-all-done = f32[1,64,4,384]{3,2,0,1:T(4,128)S(1)} async-done(((f32[1,64,4,384]{3,2,0,1:T(4,128)}), f32[1,64,4,384]{3,2,0,1:T(4,128)S(1)}, u32[]{:S(2)}, u32[]{:S(2)}) %all-to-all-start) | async-done | bytes 393248 | tf_op jit(solution)/shard_map/all_to_all | solution.py:54
  363.6 0.1 reduce_sum.35
  363.7 0.1 reduce_sum.36
  363.8 0.1 fusion.18
  363.9 55.5 %psum.7 = f32[2]{0:T(128)S(1)} all-reduce(f32[2]{0:T(128)S(1)} %fusion.18), channel_id=1, replica_groups=mesh['blk'=64,'freq'=8] {'freq'}, use_global_device_ids=true, to_apply=%region_5.6 | all-reduce | flops 2 | bytes 16 | tf_op jit(solution)/shard_map/psum | solution.py:59
  419.5 0.1 fusion.19
  419.5 0.6 copy.30
  (13 shorter events, 0.1 us)
Async XLA Ops:
  6.5 328.5 %copy-start = (bf16[1,2,16,16384]{3,2,1,0:T(8,128)(2,1)S(1)}, bf16[1,2,16,16384]{3,2,1,0:T(8,128)(2,1)}, u32[]{:S(2)}) copy-start(bf16[1,2,16,16384]{3,2,1,0:T(8,128)(2,1)} %param.8) | copy-start | bytes 3145732
  6.5 328.5 %all-gather.2.cloned.1.call-start = ((), (), s32[]{:S(2)}) async-start(), calls=%async_computation.1 | async-start | bytes 12779520 | tf_op jit(solution)/shard_map/all_gather | solution.py:36
  345.5 18.1 %all-to-all-start = ((f32[1,64,4,384]{3,2,0,1:T(4,128)}), f32[1,64,4,384]{3,2,0,1:T(4,128)S(1)}, u32[]{:S(2)}, u32[]{:S(2)}) async-start(f32[1,64,4,384]{3,2,0,1:T(4,128)} %copy.29), calls=%async_computation | async-start | bytes 786432 | tf_op jit(solution)/shard_map/all_to_all | solution.py:54
Sparse Core Ops, SparseCore 0:
  9.4 325.6 all-gather.1
where the time goes:
time: 427 us
  waiting for transfers between devices  334 us (78%)
  blocking collectives  55.5 us (13%)
  between operations  14.9 us (3%)
  matrix products  9.13 us (2%)
  starting transfers between devices  6.63 us (2%)
    all_gather x1, waiting for transfers between devices, local(): lax.all_gather(masked, 'blk', axis=3, tiled=True)  323 us
    psum x1, blocking collectives, local(): total_energy = lax.psum(local_energy, 'freq')  55.5 us
    all_to_all x1, waiting for transfers between devices, local(): lax.all_to_all(outgoing, 'blk', split_axis=1, concat_axis=1, tiled=True)  10.9 us
  transfers between devices with their start and end apart: 2, of which 2 were waited for; matrix products, arithmetic and copies ran while one was open for 1% of the time, Pallas kernels for 0%

commit v1 on v0

v1 whole, which is shorter than its diff:
```python
import jax
import jax.numpy as jnp
from jax import lax
from jax.experimental import pallas as pl
from jax.experimental.pallas import tpu as pltpu
from jax.sharding import PartitionSpec as P

RAMP = 24
NY, NX, NZ = 8, 4, 2
MESH = pl.DeviceIdType.MESH
F32 = jnp.float32
NT = (((1,), (1,)), ((), ()))
NN = (((1,), (0,)), ((), ()))


def make_kernel(n_freq, r_dev, src, k_dev):
    n_plane = NX * NZ
    rows = n_plane * r_dev
    n_bins = 2 * NY * n_plane
    half = NY // 2
    tail = src - 128

    def kernel(rec, mir, live_hbm, bins_hbm, wts_hbm, lo_hbm, hi_hbm, gain_hbm, out,
               live, bins, wts, lo, hi, gain, raw, sbuf, rbuf, meta, mapt, tap, acc, asend, abuf, bsend, bbuf, esend, ebuf,
               l_sem, p_sem, s_send, s_recv, r_send, r_recv, m_send, m_recv,
               a_send, a_recv, b_send, b_recv, e_send, e_recv):
        blk = lax.axis_index("blk")
        frq = lax.axis_index("freq")
        y = blk // n_plane
        p = blk % n_plane
        x = p // NZ
        z = p % NZ

        load = pltpu.make_async_copy(mir.at[0], raw, l_sem)
        load.start()
        small = [(live_hbm, live), (bins_hbm, bins), (wts_hbm, wts), (lo_hbm, lo), (hi_hbm, hi), (gain_hbm, gain)]
        small = [pltpu.make_async_copy(a, b, p_sem.at[i]) for i, (a, b) in enumerate(small)]
        for copy in small:
            copy.start()

        offsets = [(dx, dz) for dx in range(NX) for dz in range(NZ) if dx or dz]

        def plane_of(dx, dz):
            return ((x + dx) % NX) * NZ + (z + dz) % NZ

        peers = [plane_of(dx, dz) for dx, dz in offsets]
        y_of = [(y + d) % NY for d in range(NY)]
        f_of = [(frq + d) % n_freq for d in range(n_freq)]

        barrier = pltpu.get_barrier_semaphore()
        for q in peers:
            pl.semaphore_signal(barrier, inc=1, device_id=(y * n_plane + q, frq), device_id_type=MESH)
        for d in range(1, NY):
            pl.semaphore_signal(barrier, inc=1, device_id=(y_of[d] * n_plane + p, frq), device_id_type=MESH)
        for d in range(1, n_freq):
            pl.semaphore_signal(barrier, inc=1, device_id=(blk, f_of[d]), device_id_type=MESH)

        for copy in small:
            copy.wait()

        def column(line):
            line = jnp.broadcast_to(line.astype(F32), (r_dev, r_dev))
            on = lax.broadcasted_iota(jnp.int32, (r_dev, r_dev), 0) == lax.broadcasted_iota(jnp.int32, (r_dev, r_dev), 1)
            return jnp.sum(jnp.where(on, line, 0.0), axis=1, keepdims=True)

        lane = lax.broadcasted_iota(jnp.int32, (r_dev, 128), 1)
        table = jnp.zeros((r_dev, 128), F32)
        for i, line in enumerate([bins[0:1], bins[1:2], wts[0:1], wts[1:2], lo[...], hi[...]]):
            table = jnp.where(lane == i, column(line), table)
        mine = pl.ds(pl.multiple_of(p * r_dev, r_dev), r_dev)
        meta[mine, :] = table

        load.wait()
        on = lax.broadcasted_iota(jnp.int32, (src, k_dev), 1) < live[...]
        for c in range(2):
            sbuf[y, c] = jnp.where(on, raw[c], jnp.zeros_like(raw[c]))

        pl.semaphore_wait(barrier, len(peers) + NY - 1 + n_freq - 1)

        def ring(way, step, c):
            owner = (y - step) % NY if way == 0 else (y + step) % NY
            to = y_of[1] if way == 0 else y_of[NY - 1]
            i = step * 2 + c
            return pltpu.make_async_remote_copy(
                src_ref=sbuf.at[owner, c], dst_ref=sbuf.at[owner, c],
                send_sem=s_send.at[way, i], recv_sem=s_recv.at[way, i],
                device_id=(to * n_plane + p, frq), device_id_type=MESH)

        def landed(way, step, c):
            owner = (y - step - 1) % NY if way == 0 else (y + step + 1) % NY
            i = step * 2 + c
            pltpu.make_async_remote_copy(
                src_ref=sbuf.at[owner, c], dst_ref=sbuf.at[owner, c],
                send_sem=s_send.at[way, i], recv_sem=s_recv.at[way, i],
                device_id=(y_of[1] * n_plane + p, frq), device_id_type=MESH).wait_recv()

        for c in range(2):
            for way in range(2):
                ring(way, 0, c if way == 0 else 1 - c).start()

        def send_rows(d, carry):
            yy = (y + d) % NY
            at = (yy * n_plane) * k_dev
            for i, q in enumerate(peers):
                cols = pl.ds(pl.multiple_of(at + q * k_dev, k_dev), k_dev)
                pltpu.make_async_remote_copy(
                    src_ref=rec.at[0, :, :, cols], dst_ref=rbuf.at[yy, :, mine, :],
                    send_sem=r_send, recv_sem=r_recv.at[yy],
                    device_id=(y * n_plane + q, frq), device_id_type=MESH).start()
            cols = pl.ds(pl.multiple_of(at + p * k_dev, k_dev), k_dev)
            pltpu.make_async_copy(rec.at[0, :, :, cols], rbuf.at[yy, :, mine, :], r_recv.at[yy]).start()
            return carry

        lax.fori_loop(0, NY, send_rows, 0)

        def meta_copy(i):
            return pltpu.make_async_remote_copy(
                src_ref=meta.at[mine, :], dst_ref=meta.at[mine, :],
                send_sem=m_send.at[i], recv_sem=m_recv.at[i],
                device_id=(y * n_plane + peers[i], frq), device_id_type=MESH)

        for i in range(len(peers)):
            meta_copy(i).start()

        def pass_on(step):
            for c in range(2):
                for way in range(2):
                    part = c if way == 0 else 1 - c
                    if step + 1 < half or c == 0:
                        landed(way, step, part)
                    if step + 1 < half - 1 or (step + 1 == half - 1 and c == 0):
                        ring(way, step + 1, part).start()

        def from_peer(i):
            dx, dz = offsets[i]
            q = plane_of(-dx, -dz)
            rows_q = pl.ds(pl.multiple_of(q * r_dev, r_dev), r_dev)
            pltpu.make_async_remote_copy(
                src_ref=meta.at[rows_q, :], dst_ref=meta.at[rows_q, :],
                send_sem=m_send.at[i], recv_sem=m_recv.at[i],
                device_id=(y * n_plane + peers[i], frq), device_id_type=MESH).wait_recv()

        pass_on(0)
        for i in range(len(peers)):
            from_peer(i)
        info = meta[...]
        place = lax.broadcasted_iota(jnp.int32, (rows, n_bins), 1)
        per = 2 * NY
        named = (place % per // 2) * (2 * n_plane) + (place // per) * 2 + place % 2
        named = named.astype(F32)
        spread = jnp.where(info[:, 0:1] == named, info[:, 2:3], 0.0) + jnp.where(info[:, 1:2] == named, info[:, 3:4], 0.0)
        mapt[...] = spread.T
        at = lax.broadcasted_iota(jnp.int32, (rows, src), 1).astype(F32)
        rise = jnp.clip((at - info[:, 4:5] + 1.0) / RAMP, 0.0, 1.0)
        fall = jnp.clip((info[:, 5:6] - at) / RAMP, 0.0, 1.0)
        tap[...] = rise * fall
        for step in range(1, half - 1):
            pass_on(step)

        def product(d, first=False):
            yy = y_of[d % NY]
            left = rbuf[yy].reshape(2 * rows, k_dev)
            for c in range(2):
                part = lax.dot_general(left, sbuf[yy, c], NT, preferred_element_type=F32)
                if first:
                    acc[c] = part
                else:
                    acc[c] += part

        def rows_landed(d):
            yy = y_of[d % NY]
            pltpu.make_async_copy(rbuf.at[yy], rbuf.at[yy], r_recv.at[yy]).wait()

        for i, d in enumerate([0] + [s * k for k in range(1, half) for s in (1, -1)]):
            rows_landed(d)
            product(d, first=i == 0)
        rows_landed(half)
        pass_on(half - 1)
        product(half)

        binned = []
        for c in range(2):
            if c == 0:
                value = acc[0, 0:rows] - acc[1, rows:2 * rows]
            else:
                value = acc[1, 0:rows] + acc[0, rows:2 * rows]
            binned.append(lax.dot_general(mapt[...], value * tap[...], NN, precision=lax.Precision.HIGHEST, preferred_element_type=F32))
        asend[:, 0:128] = binned[0][:, 0:128]
        asend[:, 128:256] = binned[1][:, 0:128]
        asend[:, 256:256 + tail] = binned[0][:, 128:src]
        asend[:, 256 + tail:256 + 2 * tail] = binned[1][:, 128:src]

        def a_copy(i):
            to = pl.ds(pl.multiple_of(peers[i] * per, per), per)
            return pltpu.make_async_remote_copy(
                src_ref=asend.at[to, :], dst_ref=abuf.at[i],
                send_sem=a_send.at[i], recv_sem=a_recv.at[i],
                device_id=(y * n_plane + peers[i], frq), device_id_type=MESH)

        for i in range(len(peers)):
            a_copy(i).start()
        total = asend[pl.ds(pl.multiple_of(p * per, per), per), :]
        for i in range(len(peers)):
            a_copy(i).wait_recv()
            total = total + abuf[i]

        bsend[...] = jnp.zeros_like(bsend)
        for d in range(NY):
            for k in range(3):
                bsend[d, 2 * k:2 * k + 2, :] = total[2 * d:2 * d + 2, 128 * k:128 * k + 128]

        def b_copy(d):
            return pltpu.make_async_remote_copy(
                src_ref=bsend.at[y_of[d]], dst_ref=bbuf.at[d - 1],
                send_sem=b_send.at[d - 1], recv_sem=b_recv.at[d - 1],
                device_id=(y_of[d] * n_plane + p, frq), device_id_type=MESH)

        for d in range(1, NY):
            b_copy(d).start()
        tile = bsend[y]
        for d in range(1, NY):
            b_copy(d).wait_recv()
            tile = tile + bbuf[d - 1]
        scaled = tile * gain[...]
        square = scaled * scaled
        esend[...] = square

        def e_copy(d):
            return pltpu.make_async_remote_copy(
                src_ref=esend, dst_ref=ebuf.at[d - 1],
                send_sem=e_send.at[d - 1], recv_sem=e_recv.at[d - 1],
                device_id=(blk, f_of[d]), device_id_type=MESH)

        for d in range(1, n_freq):
            e_copy(d).start()
        for way in range(2):
            for step in range(half):
                for c in range(2):
                    part = c if way == 0 else 1 - c
                    if step < half - 1 or c == 0:
                        ring(way, step, part).wait_send()
        pltpu.make_async_copy(rbuf.at[:, :, pl.ds(0, rows - r_dev), :], rbuf.at[:, :, pl.ds(0, rows - r_dev), :], r_send).wait()
        for i in range(len(peers)):
            meta_copy(i).wait_send()
            a_copy(i).wait_send()
        for d in range(1, NY):
            b_copy(d).wait_send()
        for d in range(1, n_freq):
            e_copy(d).wait_recv()
            square = square + ebuf[d - 1]
        for d in range(1, n_freq):
            e_copy(d).wait_send()
        energy = jnp.sum(square[0:2] + square[2:4] + square[4:6], axis=1, keepdims=True)
        norm = jnp.sqrt(energy / (n_freq * 2 * src) + 1e-06)
        for c in range(2):
            out[0, c, :, 0:128] = scaled[2 * c:2 * c + 2] / norm
            out[0, c, :, 128:src] = scaled[4:6, c * tail:(c + 1) * tail] / norm

    return kernel


def solution(mesh):
    n_freq = mesh.shape["freq"]

    def local(recorded, mirror, live_counts, bins, bin_weight, taper_lo, taper_hi, gain):
        r_dev = recorded.shape[2]
        src, k_dev = mirror.shape[2], mirror.shape[3]
        n_plane = NX * NZ
        rows, per, n_peer, half = n_plane * r_dev, 2 * NY, n_plane - 1, NY // 2
        hbm, vmem = (pl.BlockSpec(memory_space=m) for m in (pltpu.HBM, pltpu.VMEM))
        dma = pltpu.SemaphoreType.DMA
        bf16 = jnp.bfloat16
        return pl.pallas_call(
            make_kernel(n_freq, r_dev, src, k_dev),
            out_shape=jax.ShapeDtypeStruct((1, 2, 2, src), F32),
            in_specs=[hbm] * 8,
            out_specs=vmem,
            scratch_shapes=[
                pltpu.VMEM((1, 1), jnp.int32),
                pltpu.VMEM((2, r_dev), jnp.int32),
                pltpu.VMEM((2, r_dev), F32),
                pltpu.VMEM((1, r_dev), jnp.int32),
                pltpu.VMEM((1, r_dev), jnp.int32),
                pltpu.VMEM((1, 1), F32),
                pltpu.VMEM((2, src, k_dev), bf16),
                pltpu.VMEM((NY, 2, src, k_dev), bf16),
                pltpu.VMEM((NY, 2, rows, k_dev), bf16),
                pltpu.VMEM((rows, 128), F32),
                pltpu.VMEM((2 * NY * n_plane, rows), F32),
                pltpu.VMEM((rows, src), F32),
                pltpu.VMEM((2, 2 * rows, src), F32),
                pltpu.VMEM((per * n_plane, 2 * src), F32),
                pltpu.VMEM((n_peer, per, 2 * src), F32),
                pltpu.VMEM((NY, 8, 128), F32),
                pltpu.VMEM((NY - 1, 8, 128), F32),
                pltpu.VMEM((8, 128), F32),
                pltpu.VMEM((n_freq - 1, 8, 128), F32),
                dma, dma((6,)),
                dma((2, 2 * half)), dma((2, 2 * half)),
                dma, dma((NY,)),
                dma((n_peer,)), dma((n_peer,)),
                dma((n_peer,)), dma((n_peer,)),
                dma((NY - 1,)), dma((NY - 1,)),
                dma((n_freq - 1,)), dma((n_freq - 1,)),
            ],
            compiler_params=pltpu.CompilerParams(
                collective_id=0, has_side_effects=True, vmem_limit_bytes=63 * 1024 * 1024
            ),
        )(recorded, mirror, live_counts, bins[0].T, bin_weight[0].T, taper_lo, taper_hi, gain.reshape(1, 1))

    in_specs = (
        P("freq", None, "blk", None),
        P("freq", None, None, "blk"),
        P("freq", "blk"),
        P("freq", "blk", None),
        P("freq", "blk", None),
        P("freq", "blk"),
        P("freq", "blk"),
        P("freq"),
    )
    out_specs = P("freq", None, "blk", None)
    return jax.shard_map(local, mesh=mesh, in_specs=in_specs, out_specs=out_specs, check_vma=False)
```

time: 427 us -> 57.3 us (0.13)
  waiting for transfers between devices: 334 us -> 0 us
  blocking collectives: 55.5 us -> 0 us
  Pallas kernels: 0 us -> 54.5 us
  between operations: 14.9 us -> 1.3 us
  matrix products: 9.13 us -> 0 us
  starting transfers between devices: 6.63 us -> 0 us
    all_gather x1 -> x0, waiting for transfers between devices: 323 us -> none  [local(): lax.all_gather(masked, 'blk', axis=3, tiled=True)]
    psum x1 -> x0, blocking collectives: 55.5 us -> none  [local(): total_energy = lax.psum(local_energy, 'freq')]
    pallas_call x0 -> x1, Pallas kernels: none -> 54.5 us  [local(): pl.pallas_call(make_kernel(n_freq, r_dev, src, k_dev), out_shape=jax.Shap...]
    all_to_all x1 -> x0, waiting for transfers between devices: 10.9 us -> none  [local(): lax.all_to_all(outgoing, 'blk', split_axis=1, concat_axis=1, tiled=True)]
    dot_general x2 -> x0, matrix products: 9.13 us -> none  [the longest x1 8.53 us: local(): jnp.einsum('fark,fbsk->farbs', recorded, lax.all_gather(masked, 'blk', ax...]
    all_to_all x1 -> x0, starting transfers between devices: 6.63 us -> none  [local(): lax.all_to_all(outgoing, 'blk', split_axis=1, concat_axis=1, tiled=True)]
  transfers between devices with their start and end apart: 2 -> 0, of which waited for: 2 -> 0; matrix products, arithmetic and copies ran while one was open for 1% -> 0% of each run, Pallas kernels for 0% -> 0%
where the time goes in v1:
time: 57.3 us; the launch traced here: 57.1 us
  Pallas kernels  54.5 us (95%)
  between operations  1.3 us (2%)
  local copies, waits for them, and re-layouts  1.28 us (2%)
    pallas_call x1, Pallas kernels, local(): pl.pallas_call(make_kernel(n_freq, r_dev, src, k_dev), out_shape=jax.Shap...  54.5 us
    unnamed x1, local copies, waits for them, and re-layouts  1.28 us

profile of v1, /device:TPU:1, one launch (start us, length us, event | category | flops | bytes accessed | tf_op | source)
XLA Modules:
  0.0 57.1 jit_solution(2789265299739286541)
XLA Ops:
  1.3 54.5 %shard_map.82 = f32[1,2,2,192]{3,2,1,0:T(2,128)} custom-call(bf16[1,2,16,16384]{3,2,1,0:T(8,128)(2,1)} %rec.1, bf16[1,2,192,256]{3,2,1,0:T(8,128)(2,1)} %mir.1, s32[1,1]{1,0:T(1,128)S(6)} %copy.10.live_hbm, s32[2,16]{1,0:T(2,128)} %bitcast.8, f32[2,16]{1,0:T(2,128)} %bitcast.9, s32[1,16]{1,0:T(1,128)} %lo_hbm.1, s32[1,16]{1,0:T(1,128)} %hi_hbm.1, ...), custom_call_target="tpu_custom_call" | custom-call | tf_op jit(solution)/shard_map/pallas_call | solution.py:273
  55.8 1.3 %copy.12 = f32[1,2,2,192]{3,2,1,0:T(2,128)} copy(f32[1,2,2,192]{3,2,1,0:T(2,128)} %shard_map.82) | data formatting | bytes 6144

commit v2 on v1

--- a/solution.py
+++ b/solution.py
@@ -6,7 +6,7 @@
 from jax.sharding import PartitionSpec as P
 
 RAMP = 24
-NY, NX, NZ = 8, 4, 2
+NY, NX, NZ, NC = 8, 4, 2, 2
 MESH = pl.DeviceIdType.MESH
 F32 = jnp.float32
 NT = (((1,), (1,)), ((), ()))
@@ -22,7 +22,7 @@
 
     def kernel(rec, mir, live_hbm, bins_hbm, wts_hbm, lo_hbm, hi_hbm, gain_hbm, out,
                live, bins, wts, lo, hi, gain, raw, sbuf, rbuf, meta, mapt, tap, acc, asend, abuf, bsend, bbuf, esend, ebuf,
-               l_sem, p_sem, s_send, s_recv, r_send, r_recv, m_send, m_recv,
+               l_sem, p_sem, word, s_send, s_recv, r_send, r_recv, m_send, m_recv,
                a_send, a_recv, b_send, b_recv, e_send, e_recv):
         blk = lax.axis_index("blk")
         frq = lax.axis_index("freq")
@@ -31,12 +31,9 @@
         x = p // NZ
         z = p % NZ
 
-        load = pltpu.make_async_copy(mir.at[0], raw, l_sem)
-        load.start()
-        small = [(live_hbm, live), (bins_hbm, bins), (wts_hbm, wts), (lo_hbm, lo), (hi_hbm, hi), (gain_hbm, gain)]
-        small = [pltpu.make_async_copy(a, b, p_sem.at[i]) for i, (a, b) in enumerate(small)]
-        for copy in small:
-            copy.start()
+        core = frq % NC
+        deep = (frq // NC) * NZ + z
+        nz = (n_freq // NC) * NZ
 
         offsets = [(dx, dz) for dx in range(NX) for dz in range(NZ) if dx or dz]
 
@@ -47,35 +44,34 @@
         y_of = [(y + d) % NY for d in range(NY)]
         f_of = [(frq + d) % n_freq for d in range(n_freq)]
 
+        near_y = [(y_of[d] * n_plane + p, frq) for d in sorted({1, NY - 1})]
+        near = []
+        for d in sorted({1 % NX, NX - 1} - {0}):
+            near.append((y * n_plane + ((x + d) % NX) * NZ + z, frq))
+        for d in sorted({1 % nz, nz - 1} - {0}):
+            at = (deep + d) % nz
+            near.append((y * n_plane + x * NZ + at % NZ, (at // NZ) * NC + core))
+        if NC == 2:
+            near.append((blk, frq - core + 1 - core))
+
         barrier = pltpu.get_barrier_semaphore()
-        for q in peers:
-            pl.semaphore_signal(barrier, inc=1, device_id=(y * n_plane + q, frq), device_id_type=MESH)
-        for d in range(1, NY):
-            pl.semaphore_signal(barrier, inc=1, device_id=(y_of[d] * n_plane + p, frq), device_id_type=MESH)
-        for d in range(1, n_freq):
-            pl.semaphore_signal(barrier, inc=1, device_id=(blk, f_of[d]), device_id_type=MESH)
-
-        for copy in small:
-            copy.wait()
-
-        def column(line):
-            line = jnp.broadcast_to(line.astype(F32), (r_dev, r_dev))
-            on = lax.broadcasted_iota(jnp.int32, (r_dev, r_dev), 0) == lax.broadcasted_iota(jnp.int32, (r_dev, r_dev), 1)
-            return jnp.sum(jnp.where(on, line, 0.0), axis=1, keepdims=True)
-
-        lane = lax.broadcasted_iota(jnp.int32, (r_dev, 128), 1)
-        table = jnp.zeros((r_dev, 128), F32)
-        for i, line in enumerate([bins[0:1], bins[1:2], wts[0:1], wts[1:2], lo[...], hi[...]]):
-            table = jnp.where(lane == i, column(line), table)
-        mine = pl.ds(pl.multiple_of(p * r_dev, r_dev), r_dev)
-        meta[mine, :] = table
-
-        load.wait()
+        for to in near_y + near:
+            pl.semaphore_signal(barrier, inc=1, device_id=to, device_id_type=MESH)
+
+        loads = [pltpu.make_async_copy(mir.at[0, c], raw.at[c], l_sem.at[c]) for c in range(2)]
+        small = [(live_hbm, live), (bins_hbm, bins), (wts_hbm, wts), (lo_hbm, lo), (hi_hbm, hi), (gain_hbm, gain)]
+        small = [pltpu.make_async_copy(a, b, p_sem.at[i]) for i, (a, b) in enumerate(small)]
+        small[0].start()
+        for copy in loads + small[1:]:
+            copy.start()
+
+        small[0].wait()
         on = lax.broadcasted_iota(jnp.int32, (src, k_dev), 1) < live[...]
         for c in range(2):
+            loads[c].wait()
             sbuf[y, c] = jnp.where(on, raw[c], jnp.zeros_like(raw[c]))
 
-        pl.semaphore_wait(barrier, len(peers) + NY - 1 + n_freq - 1)
+        pl.semaphore_wait(barrier, len(near_y) + len(near))
 
         def ring(way, step, c):
             owner = (y - step) % NY if way == 0 else (y + step) % NY
@@ -97,6 +93,35 @@
         for c in range(2):
             for way in range(2):
                 ring(way, 0, c if way == 0 else 1 - c).start()
+
+        def tell(i):
+            for to in near:
+                pl.semaphore_signal(word.at[i], inc=1, device_id=to, device_id_type=MESH)
+
+        def heard(i):
+            pl.semaphore_wait(word.at[i], len(near))
+
+        tell(0)
+
+        for copy in small[1:]:
+            copy.wait()
+
+        def column(line):
+            line = jnp.broadcast_to(line.astype(F32), (r_dev, r_dev))
+            on = lax.broadcasted_iota(jnp.int32, (r_dev, r_dev), 0) == lax.broadcasted_iota(jnp.int32, (r_dev, r_dev), 1)
+            return jnp.sum(jnp.where(on, line, 0.0), axis=1, keepdims=True)
+
+        lane = lax.broadcasted_iota(jnp.int32, (r_dev, 128), 1)
+        table = jnp.zeros((r_dev, 128), F32)
+        for i, line in enumerate([bins[0:1], bins[1:2], wts[0:1], wts[1:2], lo[...], hi[...]]):
+            table = jnp.where(lane == i, column(line), table)
+        mine = pl.ds(pl.multiple_of(p * r_dev, r_dev), r_dev)
+        meta[mine, :] = table
+
+        heard(0)
+        tell(1)
+        heard(1)
+        tell(2)
 
         def send_rows(d, carry):
             yy = (y + d) % NY
@@ -111,7 +136,12 @@
             pltpu.make_async_copy(rec.at[0, :, :, cols], rbuf.at[yy, :, mine, :], r_recv.at[yy]).start()
             return carry
 
-        lax.fori_loop(0, NY, send_rows, 0)
+        def send_part(i):
+            ends = [0, 3, 6, NY] if half == 4 else [0, NY]
+            if i < len(ends) - 1:
+                lax.fori_loop(ends[i], ends[i + 1], send_rows, 0)
+
+        send_part(0)
 
         def meta_copy(i):
             return pltpu.make_async_remote_copy(
@@ -130,6 +160,8 @@
                         landed(way, step, part)
                     if step + 1 < half - 1 or (step + 1 == half - 1 and c == 0):
                         ring(way, step + 1, part).start()
+                if c == 0:
+                    send_part(step + 1)
 
         def from_peer(i):
             dx, dz = offsets[i]
@@ -141,6 +173,8 @@
                 device_id=(y * n_plane + peers[i], frq), device_id_type=MESH).wait_recv()
 
         pass_on(0)
+        heard(2)
+        tell(3)
         for i in range(len(peers)):
             from_peer(i)
         info = meta[...]
@@ -156,6 +190,7 @@
         tap[...] = rise * fall
         for step in range(1, half - 1):
             pass_on(step)
+        heard(3)
 
         def product(d, first=False):
             yy = y_of[d % NY]
@@ -295,7 +330,7 @@
                 pltpu.VMEM((NY - 1, 8, 128), F32),
                 pltpu.VMEM((8, 128), F32),
                 pltpu.VMEM((n_freq - 1, 8, 128), F32),
-                dma, dma((6,)),
+                dma((2,)), dma((6,)), pltpu.SemaphoreType.REGULAR((4,)),
                 dma((2, 2 * half)), dma((2, 2 * half)),
                 dma, dma((NY,)),
                 dma((n_peer,)), dma((n_peer,)),

time: 57.3 us -> 53.3 us (0.930)
  Pallas kernels: 54.5 us -> 50.5 us
    pallas_call x1, Pallas kernels: 54.5 us -> 50.5 us  [local(): pl.pallas_call(make_kernel(n_freq, r_dev, src, k_dev), out_shape=jax.Shap...]
where the time goes in v2:
time: 53.3 us; the launch traced here: 53.1 us
  Pallas kernels  50.5 us (95%)
  between operations  1.3 us (2%)
  local copies, waits for them, and re-layouts  1.28 us (2%)
    pallas_call x1, Pallas kernels, local(): pl.pallas_call(make_kernel(n_freq, r_dev, src, k_dev), out_shape=jax.Shap...  50.5 us
    unnamed x1, local copies, waits for them, and re-layouts  1.28 us

profile of v2, /device:TPU:1, one launch (start us, length us, event | category | flops | bytes accessed | tf_op | source)
XLA Modules:
  0.0 53.1 jit_solution(12607717129938343391)
XLA Ops:
  1.3 50.5 %shard_map.82 = f32[1,2,2,192]{3,2,1,0:T(2,128)} custom-call(bf16[1,2,16,16384]{3,2,1,0:T(8,128)(2,1)} %rec.1, bf16[1,2,192,256]{3,2,1,0:T(8,128)(2,1)} %mir.1, s32[1,1]{1,0:T(1,128)S(6)} %copy.10.live_hbm, s32[2,16]{1,0:T(2,128)} %bitcast.8, f32[2,16]{1,0:T(2,128)} %bitcast.9, s32[1,16]{1,0:T(1,128)} %lo_hbm.1, s32[1,16]{1,0:T(1,128)} %hi_hbm.1, ...), custom_call_target="tpu_custom_call" | custom-call | tf_op jit(solution)/shard_map/pallas_call | solution.py:308
  51.8 1.3 %copy.12 = f32[1,2,2,192]{3,2,1,0:T(2,128)} copy(f32[1,2,2,192]{3,2,1,0:T(2,128)} %shard_map.82) | data formatting | bytes 6144

commit v3 on v2

v3 whole, which is shorter than its diff:
```python
import jax
import jax.numpy as jnp
from jax import lax
from jax.experimental import pallas as pl
from jax.experimental.pallas import tpu as pltpu
from jax.sharding import PartitionSpec as P

RAMP = 24
CUTS = 1
NY, NX, NZ, NC = 8, 4, 2, 2
MESH = pl.DeviceIdType.MESH
F32 = jnp.float32
NT = (((1,), (1,)), ((), ()))
NN = (((1,), (0,)), ((), ()))


def far_first(n):
    return sorted(range(1, n), key=lambda d: -min(d, n - d))


def make_kernel(n_freq, r_dev, src, k_dev):
    n_plane = NX * NZ
    rows = n_plane * r_dev
    n_bins = 2 * NY * n_plane
    half = NY // 2
    tail = src - 128

    def kernel(rec, mir, live_hbm, bins_hbm, wts_hbm, lo_hbm, hi_hbm, gain_hbm, out,
               live, bins, wts, lo, hi, gain, raw, sbuf, rraw, rsend, rbuf, meta, mapt, tap, acc, asend, abuf, bsend, bbuf, esend, ebuf,
               l_sem, p_sem, q_sem, word_p, word_f, s_send, s_recv, r_send, r_recv, m_send, m_recv,
               a_send, a_recv, b_send, b_recv, e_send, e_recv):
        blk = lax.axis_index("blk")
        frq = lax.axis_index("freq")
        y = blk // n_plane
        p = blk % n_plane
        x = p // NZ
        z = p % NZ

        core = frq % NC
        deep = (frq // NC) * NZ + z
        nz = (n_freq // NC) * NZ

        offsets = [(dx, dz) for dx in range(NX) for dz in range(NZ) if dx or dz]
        offsets.sort(key=lambda o: min(o[0], NX - o[0]) + o[1])

        def plane_of(dx, dz):
            return ((x + dx) % NX) * NZ + (z + dz) % NZ

        peers = [plane_of(dx, dz) for dx, dz in offsets]
        y_of = [(y + d) % NY for d in range(NY)]
        f_of = [(frq + d) % n_freq for d in range(n_freq)]

        near_y = [(y_of[d] * n_plane + p, frq) for d in (1, NY - 1)]
        near_plane = []
        for d in sorted({1 % NX, NX - 1} - {0}):
            near_plane.append((y * n_plane + ((x + d) % NX) * NZ + z, frq))
        if NZ == 2:
            near_plane.append((y * n_plane + x * NZ + 1 - z, frq))
        near_freq = []
        for d in sorted({1 % nz, nz - 1} - {0}):
            at = (deep + d) % nz
            near_freq.append((y * n_plane + x * NZ + at % NZ, (at // NZ) * NC + core))
        if NC == 2:
            near_freq.append((blk, frq - core + 1 - core))

        barrier = pltpu.get_barrier_semaphore()
        for to in near_y + near_plane + near_freq:
            pl.semaphore_signal(barrier, inc=1, device_id=to, device_id_type=MESH)

        loads = [pltpu.make_async_copy(mir.at[0, c], raw.at[c], l_sem.at[c]) for c in range(2)]
        small = [(live_hbm, live), (bins_hbm, bins), (wts_hbm, wts), (lo_hbm, lo), (hi_hbm, hi), (gain_hbm, gain)]
        small = [pltpu.make_async_copy(a, b, p_sem.at[i]) for i, (a, b) in enumerate(small)]
        small[0].start()
        rows_in = pltpu.make_async_copy(rec.at[0], rraw, q_sem)
        for copy in loads + [rows_in] + small[1:]:
            copy.start()

        small[0].wait()
        on = lax.broadcasted_iota(jnp.int32, (src, k_dev), 1) < live[...]
        for c in range(2):
            loads[c].wait()
            sbuf[y, c] = jnp.where(on, raw[c], jnp.zeros_like(raw[c]))

        pl.semaphore_wait(barrier, len(near_y) + len(near_plane) + len(near_freq))

        n_piece = 2 * CUTS
        piece = src // CUTS

        def ring(way, step, i, landing=False):
            owner = y - step - landing if way == 0 else y + step + landing
            part = i if way == 0 else n_piece - 1 - i
            ref = sbuf.at[(owner + NY) % NY, part // CUTS, pl.ds(part % CUTS * piece, piece), :]
            return pltpu.make_async_remote_copy(
                src_ref=ref, dst_ref=ref,
                send_sem=s_send.at[way, step * n_piece + i], recv_sem=s_recv.at[way, step * n_piece + i],
                device_id=near_y[way], device_id_type=MESH)

        def pieces(step):
            return n_piece // 2 if step == half - 1 else n_piece

        for i in range(n_piece):
            for way in range(2):
                ring(way, 0, i).start()

        def tell(word, near, i):
            for to in near:
                pl.semaphore_signal(word.at[i], inc=1, device_id=to, device_id_type=MESH)

        def heard(word, near, i):
            pl.semaphore_wait(word.at[i], len(near))

        tell(word_p, near_plane, 0)
        tell(word_f, near_freq, 0)

        rows_in.wait()
        for q in range(n_plane):
            for yy in range(NY):
                at = (yy * n_plane + q) * k_dev
                rsend[q, yy] = rraw[:, :, at:at + k_dev]
        rbuf[p] = rsend[p]

        def rows_copy(i, landing=False):
            dx, dz = offsets[i]
            dst = rbuf.at[plane_of(-dx, -dz) if landing else p]
            return pltpu.make_async_remote_copy(
                src_ref=dst if landing else rsend.at[peers[i]], dst_ref=dst,
                send_sem=r_send.at[i], recv_sem=r_recv.at[i],
                device_id=(y * n_plane + peers[i], frq), device_id_type=MESH)

        def hops(i):
            return min(offsets[i][0], NX - offsets[i][0]) + offsets[i][1]

        def send_rows(far):
            for i in range(len(peers)):
                if hops(i) == far:
                    rows_copy(i).start()

        send_rows(1)

        for copy in small[1:]:
            copy.wait()

        def column(line):
            line = jnp.broadcast_to(line.astype(F32), (r_dev, r_dev))
            on = lax.broadcasted_iota(jnp.int32, (r_dev, r_dev), 0) == lax.broadcasted_iota(jnp.int32, (r_dev, r_dev), 1)
            return jnp.sum(jnp.where(on, line, 0.0), axis=1, keepdims=True)

        lane = lax.broadcasted_iota(jnp.int32, (r_dev, 128), 1)
        table = jnp.zeros((r_dev, 128), F32)
        for i, line in enumerate([bins[0:1], bins[1:2], wts[0:1], wts[1:2], lo[...], hi[...]]):
            table = jnp.where(lane == i, column(line), table)
        mine = pl.ds(pl.multiple_of(p * r_dev, r_dev), r_dev)
        meta[mine, :] = table

        def meta_copy(i):
            return pltpu.make_async_remote_copy(
                src_ref=meta.at[mine, :], dst_ref=meta.at[mine, :],
                send_sem=m_send.at[i], recv_sem=m_recv.at[i],
                device_id=(y * n_plane + peers[i], frq), device_id_type=MESH)

        def pass_on(step):
            for i in range(pieces(step)):
                for way in range(2):
                    ring(way, step, i, landing=True).wait_recv()
                    if step + 1 < half and i < pieces(step + 1):
                        ring(way, step + 1, i).start()

        def from_peer(i):
            dx, dz = offsets[i]
            q = plane_of(-dx, -dz)
            rows_q = pl.ds(pl.multiple_of(q * r_dev, r_dev), r_dev)
            pltpu.make_async_remote_copy(
                src_ref=meta.at[rows_q, :], dst_ref=meta.at[rows_q, :],
                send_sem=m_send.at[i], recv_sem=m_recv.at[i],
                device_id=(y * n_plane + peers[i], frq), device_id_type=MESH).wait_recv()

        pass_on(0)
        heard(word_p, near_plane, 0)
        tell(word_p, near_plane, 1)
        send_rows(2)
        if half > 2:
            pass_on(1)
        heard(word_p, near_plane, 1)
        send_rows(3)
        for i in range(len(peers)):
            meta_copy(i).start()
        heard(word_f, near_freq, 0)
        tell(word_f, near_freq, 1)
        for step in range(2, half - 1):
            pass_on(step)
        heard(word_f, near_freq, 1)
        tell(word_f, near_freq, 2)

        for i in range(len(peers)):
            from_peer(i)
        info = meta[...]
        place = lax.broadcasted_iota(jnp.int32, (rows, n_bins), 1)
        per = 2 * NY
        named = (place % per // 2) * (2 * n_plane) + (place // per) * 2 + place % 2
        named = named.astype(F32)
        spread = jnp.where(info[:, 0:1] == named, info[:, 2:3], 0.0) + jnp.where(info[:, 1:2] == named, info[:, 3:4], 0.0)
        mapt[...] = spread.T
        at = lax.broadcasted_iota(jnp.int32, (rows, src), 1).astype(F32)
        rise = jnp.clip((at - info[:, 4:5] + 1.0) / RAMP, 0.0, 1.0)
        fall = jnp.clip((info[:, 5:6] - at) / RAMP, 0.0, 1.0)
        tap[...] = rise * fall

        for i in range(len(peers)):
            rows_copy(i, landing=True).wait_recv()

        def product(d, first=False):
            yy = y_of[d % NY]
            left = rbuf[:, yy].reshape(2 * rows, k_dev)
            for c in range(2):
                part = lax.dot_general(left, sbuf[yy, c], NT, preferred_element_type=F32)
                if first:
                    acc[c] = part
                else:
                    acc[c] += part

        for i, d in enumerate([0] + [s * k for k in range(1, half) for s in (1, -1)]):
            product(d, first=i == 0)
        heard(word_f, near_freq, 2)
        tell(word_f, near_freq, 3)
        pass_on(half - 1)
        product(half)

        def of(c, part):
            return acc[c].reshape(n_plane, 2, r_dev, src)[:, part].reshape(rows, src)

        binned = []
        for c in range(2):
            if c == 0:
                value = of(0, 0) - of(1, 1)
            else:
                value = of(1, 0) + of(0, 1)
            binned.append(lax.dot_general(mapt[...], value * tap[...], NN, precision=lax.Precision.HIGHEST, preferred_element_type=F32))
        asend[:, 0:128] = binned[0][:, 0:128]
        asend[:, 128:256] = binned[1][:, 0:128]
        asend[:, 256:256 + tail] = binned[0][:, 128:src]
        asend[:, 256 + tail:256 + 2 * tail] = binned[1][:, 128:src]

        def a_copy(i):
            to = pl.ds(pl.multiple_of(peers[i] * per, per), per)
            return pltpu.make_async_remote_copy(
                src_ref=asend.at[to, :], dst_ref=abuf.at[i],
                send_sem=a_send.at[i], recv_sem=a_recv.at[i],
                device_id=(y * n_plane + peers[i], frq), device_id_type=MESH)

        for i in reversed(range(len(peers))):
            a_copy(i).start()
        total = asend[pl.ds(pl.multiple_of(p * per, per), per), :]
        for i in range(len(peers)):
            a_copy(i).wait_recv()
            total = total + abuf[i]

        bsend[...] = jnp.zeros_like(bsend)
        for d in range(NY):
            for k in range(3):
                bsend[d, 2 * k:2 * k + 2, :] = total[2 * d:2 * d + 2, 128 * k:128 * k + 128]

        def b_copy(d):
            return pltpu.make_async_remote_copy(
                src_ref=bsend.at[y_of[d]], dst_ref=bbuf.at[d - 1],
                send_sem=b_send.at[d - 1], recv_sem=b_recv.at[d - 1],
                device_id=(y_of[d] * n_plane + p, frq), device_id_type=MESH)

        for d in far_first(NY):
            b_copy(d).start()
        tile = bsend[y]
        for d in range(1, NY):
            b_copy(d).wait_recv()
            tile = tile + bbuf[d - 1]
        scaled = tile * gain[...]
        square = scaled * scaled
        esend[...] = square

        def e_copy(d):
            return pltpu.make_async_remote_copy(
                src_ref=esend, dst_ref=ebuf.at[d - 1],
                send_sem=e_send.at[d - 1], recv_sem=e_recv.at[d - 1],
                device_id=(blk, f_of[d]), device_id_type=MESH)

        heard(word_f, near_freq, 3)
        for d in far_first(n_freq):
            e_copy(d).start()
        for step in range(half):
            for i in range(pieces(step)):
                for way in range(2):
                    ring(way, step, i).wait_send()
        for i in range(len(peers)):
            rows_copy(i).wait_send()
            meta_copy(i).wait_send()
            a_copy(i).wait_send()
        for d in range(1, NY):
            b_copy(d).wait_send()
        for d in range(1, n_freq):
            e_copy(d).wait_recv()
            square = square + ebuf[d - 1]
        for d in range(1, n_freq):
            e_copy(d).wait_send()
        energy = jnp.sum(square[0:2] + square[2:4] + square[4:6], axis=1, keepdims=True)
        norm = jnp.sqrt(energy / (n_freq * 2 * src) + 1e-06)
        for c in range(2):
            out[0, c, :, 0:128] = scaled[2 * c:2 * c + 2] / norm
            out[0, c, :, 128:src] = scaled[4:6, c * tail:(c + 1) * tail] / norm

    return kernel


def solution(mesh):
    n_freq = mesh.shape["freq"]

    def local(recorded, mirror, live_counts, bins, bin_weight, taper_lo, taper_hi, gain):
        r_dev = recorded.shape[2]
        src, k_dev = mirror.shape[2], mirror.shape[3]
        n_plane = NX * NZ
        rows, per, n_peer, half = n_plane * r_dev, 2 * NY, n_plane - 1, NY // 2
        hbm, vmem = (pl.BlockSpec(memory_space=m) for m in (pltpu.HBM, pltpu.VMEM))
        dma = pltpu.SemaphoreType.DMA
        bf16 = jnp.bfloat16
        return pl.pallas_call(
            make_kernel(n_freq, r_dev, src, k_dev),
            out_shape=jax.ShapeDtypeStruct((1, 2, 2, src), F32),
            in_specs=[hbm] * 8,
            out_specs=vmem,
            scratch_shapes=[
                pltpu.VMEM((1, 1), jnp.int32),
                pltpu.VMEM((2, r_dev), jnp.int32),
                pltpu.VMEM((2, r_dev), F32),
                pltpu.VMEM((1, r_dev), jnp.int32),
                pltpu.VMEM((1, r_dev), jnp.int32),
                pltpu.VMEM((1, 1), F32),
                pltpu.VMEM((2, src, k_dev), bf16),
                pltpu.VMEM((NY, 2, src, k_dev), bf16),
                pltpu.VMEM((2, r_dev, NY * n_plane * k_dev), bf16),
                pltpu.VMEM((n_plane, NY, 2, r_dev, k_dev), bf16),
                pltpu.VMEM((n_plane, NY, 2, r_dev, k_dev), bf16),
                pltpu.VMEM((rows, 128), F32),
                pltpu.VMEM((2 * NY * n_plane, rows), F32),
                pltpu.VMEM((rows, src), F32),
                pltpu.VMEM((2, 2 * rows, src), F32),
                pltpu.VMEM((per * n_plane, 2 * src), F32),
                pltpu.VMEM((n_peer, per, 2 * src), F32),
                pltpu.VMEM((NY, 8, 128), F32),
                pltpu.VMEM((NY - 1, 8, 128), F32),
                pltpu.VMEM((8, 128), F32),
                pltpu.VMEM((n_freq - 1, 8, 128), F32),
                dma((2,)), dma((6,)), dma, pltpu.SemaphoreType.REGULAR((2,)), pltpu.SemaphoreType.REGULAR((4,)),
                dma((2, 2 * CUTS * half)), dma((2, 2 * CUTS * half)),
                dma((n_peer,)), dma((n_peer,)),
                dma((n_peer,)), dma((n_peer,)),
                dma((n_peer,)), dma((n_peer,)),
                dma((NY - 1,)), dma((NY - 1,)),
                dma((n_freq - 1,)), dma((n_freq - 1,)),
            ],
            compiler_params=pltpu.CompilerParams(
                collective_id=0, has_side_effects=True, vmem_limit_bytes=55150 * 1024
            ),
        )(recorded, mirror, live_counts, bins[0].T, bin_weight[0].T, taper_lo, taper_hi, gain.reshape(1, 1))

    in_specs = (
        P("freq", None, "blk", None),
        P("freq", None, None, "blk"),
        P("freq", "blk"),
        P("freq", "blk", None),
        P("freq", "blk", None),
        P("freq", "blk"),
        P("freq", "blk"),
        P("freq"),
    )
    out_specs = P("freq", None, "blk", None)
    return jax.shard_map(local, mesh=mesh, in_specs=in_specs, out_specs=out_specs, check_vma=False)
```

time: 53.3 us -> 50.3 us (0.944)
  Pallas kernels: 50.5 us -> 47.5 us
    pallas_call x1, Pallas kernels: 50.5 us -> 47.5 us  [local(): pl.pallas_call(make_kernel(n_freq, r_dev, src, k_dev), out_shape=jax.Shap...]
    unnamed x1 -> x9, local copies, waits for them, and re-layouts: 1.28 us -> 1.28 us
where the time goes in v3:
time: 50.3 us; the launch traced here: 50.2 us
  Pallas kernels  47.5 us (94%)
  between operations  1.34 us (3%)
  local copies, waits for them, and re-layouts  1.28 us (3%)
    pallas_call x1, Pallas kernels, local(): pl.pallas_call(make_kernel(n_freq, r_dev, src, k_dev), out_shape=jax.Shap...  47.5 us
    unnamed x9, local copies, waits for them, and re-layouts  1.28 us

profile of v3, /device:TPU:1, one launch (start us, length us, event | category | flops | bytes accessed | tf_op | source)
XLA Modules:
  0.0 50.2 jit_solution(13599498773855219412)
XLA Ops:
  1.3 0.0 copy-start.1
  1.3 0.0 copy-start.3
  1.3 0.0 copy-start
  1.3 0.0 copy-start.2
  1.3 0.6 %copy-done.1 = f32[1,16,2]{1,2,0:T(2,128)S(1)} copy-done((f32[1,16,2]{1,2,0:T(2,128)S(1)}, f32[1,16,2]{1,2,0:T(2,128)}, u32[]{:S(2)}) %copy-start.1) | copy-done | bytes 152
  2.0 0.0 copy-done.3
  2.0 0.0 copy-done
  2.0 0.0 copy-done.2
  2.0 47.5 %shard_map.82 = f32[1,2,2,192]{3,2,1,0:T(2,128)S(1)} custom-call(bf16[1,2,16,16384]{3,2,1,0:T(8,128)(2,1)} %rec.1, bf16[1,2,192,256]{3,2,1,0:T(8,128)(2,1)} %mir.1, s32[1,1]{1,0:T(1,128)S(6)} %copy.10.live_hbm, s32[2,16]{1,0:T(2,128)S(1)} %bitcast.8, f32[2,16]{1,0:T(2,128)S(1)} %bitcast.9, s32[1,16]{1,0:T(1,128)S(1)} %copy-done.2, s32[1,16]{1,0:T(1,128)S(1)} %copy-done.3, ...), custom_call_target="tpu_custom_call" | custom-call | tf_op jit(solution)/shard_map/pallas_call | solution.py:322
  49.6 0.6 %copy.12 = f32[1,2,2,192]{3,2,1,0:T(2,128)} copy(f32[1,2,2,192]{3,2,1,0:T(2,128)S(1)} %shard_map.82) | data formatting | bytes 6144
Async XLA Ops:
  1.3 0.7 %copy-start.1 = (f32[1,16,2]{1,2,0:T(2,128)S(1)}, f32[1,16,2]{1,2,0:T(2,128)}, u32[]{:S(2)}) copy-start(f32[1,16,2]{1,2,0:T(2,128)} %param.12) | copy-start | bytes 388
  1.3 0.7 %copy-start.3 = (s32[1,16]{1,0:T(1,128)S(1)}, s32[1,16]{1,0:T(1,128)}, u32[]{:S(2)}) copy-start(s32[1,16]{1,0:T(1,128)} %hi_hbm.1) | copy-start | bytes 196
  1.3 0.7 %copy-start = (s32[1,16,2]{1,2,0:T(2,128)S(1)}, s32[1,16,2]{1,2,0:T(2,128)}, u32[]{:S(2)}) copy-start(s32[1,16,2]{1,2,0:T(2,128)} %param.11) | copy-start | bytes 388
  1.3 0.7 %copy-start.2 = (s32[1,16]{1,0:T(1,128)S(1)}, s32[1,16]{1,0:T(1,128)}, u32[]{:S(2)}) copy-start(s32[1,16]{1,0:T(1,128)} %lo_hbm.1) | copy-start | bytes 196

commit v4 on v3

--- a/solution.py
+++ b/solution.py
@@ -109,6 +109,7 @@
         def heard(word, near, i):
             pl.semaphore_wait(word.at[i], len(near))
 
+        bsend[...] = jnp.zeros_like(bsend)
         tell(word_p, near_plane, 0)
         tell(word_f, near_freq, 0)
 
@@ -127,15 +128,21 @@
                 send_sem=r_send.at[i], recv_sem=r_recv.at[i],
                 device_id=(y * n_plane + peers[i], frq), device_id_type=MESH)
 
+        def meta_copy(i):
+            return pltpu.make_async_remote_copy(
+                src_ref=meta.at[mine, :], dst_ref=meta.at[mine, :],
+                send_sem=m_send.at[i], recv_sem=m_recv.at[i],
+                device_id=(y * n_plane + peers[i], frq), device_id_type=MESH)
+
         def hops(i):
             return min(offsets[i][0], NX - offsets[i][0]) + offsets[i][1]
 
         def send_rows(far):
             for i in range(len(peers)):
                 if hops(i) == far:
+                    meta_copy(i).start()
                     rows_copy(i).start()
 
-        send_rows(1)
 
         for copy in small[1:]:
             copy.wait()
@@ -152,11 +159,7 @@
         mine = pl.ds(pl.multiple_of(p * r_dev, r_dev), r_dev)
         meta[mine, :] = table
 
-        def meta_copy(i):
-            return pltpu.make_async_remote_copy(
-                src_ref=meta.at[mine, :], dst_ref=meta.at[mine, :],
-                send_sem=m_send.at[i], recv_sem=m_recv.at[i],
-                device_id=(y * n_plane + peers[i], frq), device_id_type=MESH)
+        send_rows(1)
 
         def pass_on(step):
             for i in range(pieces(step)):
@@ -174,16 +177,14 @@
                 send_sem=m_send.at[i], recv_sem=m_recv.at[i],
                 device_id=(y * n_plane + peers[i], frq), device_id_type=MESH).wait_recv()
 
-        pass_on(0)
         heard(word_p, near_plane, 0)
         tell(word_p, near_plane, 1)
         send_rows(2)
+        pass_on(0)
         if half > 2:
             pass_on(1)
         heard(word_p, near_plane, 1)
         send_rows(3)
-        for i in range(len(peers)):
-            meta_copy(i).start()
         heard(word_f, near_freq, 0)
         tell(word_f, near_freq, 1)
         for step in range(2, half - 1):
@@ -205,25 +206,23 @@
         fall = jnp.clip((info[:, 5:6] - at) / RAMP, 0.0, 1.0)
         tap[...] = rise * fall
 
+
         for i in range(len(peers)):
             rows_copy(i, landing=True).wait_recv()
 
-        def product(d, first=False):
-            yy = y_of[d % NY]
-            left = rbuf[:, yy].reshape(2 * rows, k_dev)
-            for c in range(2):
-                part = lax.dot_general(left, sbuf[yy, c], NT, preferred_element_type=F32)
-                if first:
-                    acc[c] = part
-                else:
-                    acc[c] += part
-
-        for i, d in enumerate([0] + [s * k for k in range(1, half) for s in (1, -1)]):
-            product(d, first=i == 0)
+        def product(blocks):
+            at = [y_of[d % NY] for d in blocks]
+            left = jnp.concatenate([rbuf[:, yy].reshape(2 * rows, k_dev) for yy in at], axis=1)
+            return [lax.dot_general(left, jnp.concatenate([sbuf[yy, c] for yy in at], axis=1), NT, preferred_element_type=F32)
+                    for c in range(2)]
+
+        for c, part in enumerate(product([d for d in range(NY) if d != half])):
+            acc[c] = part
         heard(word_f, near_freq, 2)
         tell(word_f, near_freq, 3)
         pass_on(half - 1)
-        product(half)
+        for c, part in enumerate(product([half])):
+            acc[c] += part
 
         def of(c, part):
             return acc[c].reshape(n_plane, 2, r_dev, src)[:, part].reshape(rows, src)
@@ -254,7 +253,6 @@
             a_copy(i).wait_recv()
             total = total + abuf[i]
 
-        bsend[...] = jnp.zeros_like(bsend)
         for d in range(NY):
             for k in range(3):
                 bsend[d, 2 * k:2 * k + 2, :] = total[2 * d:2 * d + 2, 128 * k:128 * k + 128]

time: 50.3 us -> 49.5 us (0.984)
  Pallas kernels: 47.5 us -> 46.7 us
    pallas_call x1, Pallas kernels: 47.5 us -> 46.7 us  [local(): pl.pallas_call(make_kernel(n_freq, r_dev, src, k_dev), out_shape=jax.Shap...]
where the time goes in v4:
time: 49.5 us; the launch traced here: 49.3 us
  Pallas kernels  46.7 us (94%)
  between operations  1.34 us (3%)
  local copies, waits for them, and re-layouts  1.28 us (3%)
    pallas_call x1, Pallas kernels, local(): pl.pallas_call(make_kernel(n_freq, r_dev, src, k_dev), out_shape=jax.Shap...  46.7 us
    unnamed x9, local copies, waits for them, and re-layouts  1.28 us

profile of v4, /device:TPU:1, one launch (start us, length us, event | category | flops | bytes accessed | tf_op | source)
XLA Modules:
  0.0 49.3 jit_solution(13888681872001165775)
XLA Ops:
  1.3 0.0 copy-start.1
  1.3 0.0 copy-start.3
  1.3 0.0 copy-start
  1.3 0.0 copy-start.2
  1.3 0.6 %copy-done.1 = f32[1,16,2]{1,2,0:T(2,128)S(1)} copy-done((f32[1,16,2]{1,2,0:T(2,128)S(1)}, f32[1,16,2]{1,2,0:T(2,128)}, u32[]{:S(2)}) %copy-start.1) | copy-done | bytes 152
  2.0 0.0 copy-done.3
  2.0 0.0 copy-done
  2.0 0.0 copy-done.2
  2.0 46.7 %shard_map.82 = f32[1,2,2,192]{3,2,1,0:T(2,128)S(1)} custom-call(bf16[1,2,16,16384]{3,2,1,0:T(8,128)(2,1)} %rec.1, bf16[1,2,192,256]{3,2,1,0:T(8,128)(2,1)} %mir.1, s32[1,1]{1,0:T(1,128)S(6)} %copy.10.live_hbm, s32[2,16]{1,0:T(2,128)S(1)} %bitcast.8, f32[2,16]{1,0:T(2,128)S(1)} %bitcast.9, s32[1,16]{1,0:T(1,128)S(1)} %copy-done.2, s32[1,16]{1,0:T(1,128)S(1)} %copy-done.3, ...), custom_call_target="tpu_custom_call" | custom-call | tf_op jit(solution)/shard_map/pallas_call | solution.py:320
  48.7 0.6 %copy.12 = f32[1,2,2,192]{3,2,1,0:T(2,128)} copy(f32[1,2,2,192]{3,2,1,0:T(2,128)S(1)} %shard_map.82) | data formatting | bytes 6144
Async XLA Ops:
  1.3 0.7 %copy-start.1 = (f32[1,16,2]{1,2,0:T(2,128)S(1)}, f32[1,16,2]{1,2,0:T(2,128)}, u32[]{:S(2)}) copy-start(f32[1,16,2]{1,2,0:T(2,128)} %param.12) | copy-start | bytes 388
  1.3 0.7 %copy-start.3 = (s32[1,16]{1,0:T(1,128)S(1)}, s32[1,16]{1,0:T(1,128)}, u32[]{:S(2)}) copy-start(s32[1,16]{1,0:T(1,128)} %hi_hbm.1) | copy-start | bytes 196
  1.3 0.7 %copy-start = (s32[1,16,2]{1,2,0:T(2,128)S(1)}, s32[1,16,2]{1,2,0:T(2,128)}, u32[]{:S(2)}) copy-start(s32[1,16,2]{1,2,0:T(2,128)} %param.11) | copy-start | bytes 388
  1.3 0.7 %copy-start.2 = (s32[1,16]{1,0:T(1,128)S(1)}, s32[1,16]{1,0:T(1,128)}, u32[]{:S(2)}) copy-start(s32[1,16]{1,0:T(1,128)} %lo_hbm.1) | copy-start | bytes 196

commit v5 on v4

--- a/solution.py
+++ b/solution.py
@@ -218,8 +218,6 @@
 
         for c, part in enumerate(product([d for d in range(NY) if d != half])):
             acc[c] = part
-        heard(word_f, near_freq, 2)
-        tell(word_f, near_freq, 3)
         pass_on(half - 1)
         for c, part in enumerate(product([half])):
             acc[c] += part
@@ -233,7 +231,13 @@
                 value = of(0, 0) - of(1, 1)
             else:
                 value = of(1, 0) + of(0, 1)
-            binned.append(lax.dot_general(mapt[...], value * tap[...], NN, precision=lax.Precision.HIGHEST, preferred_element_type=F32))
+            value = value * tap[...]
+            top = value.astype(jnp.bfloat16)
+            low = (value - top.astype(F32)).astype(jnp.bfloat16)
+            weight_top = mapt[...].astype(jnp.bfloat16)
+            weight_low = (mapt[...] - weight_top.astype(F32)).astype(jnp.bfloat16)
+            binned.append(sum(lax.dot_general(m, v, NN, preferred_element_type=F32)
+                              for m, v in ((weight_top, low), (weight_low, top), (weight_top, top))))
         asend[:, 0:128] = binned[0][:, 0:128]
         asend[:, 128:256] = binned[1][:, 0:128]
         asend[:, 256:256 + tail] = binned[0][:, 128:src]
@@ -248,6 +252,8 @@
 
         for i in reversed(range(len(peers))):
             a_copy(i).start()
+        heard(word_f, near_freq, 2)
+        tell(word_f, near_freq, 3)
         total = asend[pl.ds(pl.multiple_of(p * per, per), per), :]
         for i in range(len(peers)):
             a_copy(i).wait_recv()

time: 49.5 us -> 49.2 us (level)
  no operation moved by 1% of the time
where the time goes in v5:
time: 49.2 us; the launch traced here: 49 us
  Pallas kernels  46.4 us (94%)
  between operations  1.34 us (3%)
  local copies, waits for them, and re-layouts  1.28 us (3%)
    pallas_call x1, Pallas kernels, local(): pl.pallas_call(make_kernel(n_freq, r_dev, src, k_dev), out_shape=jax.Shap...  46.4 us
    unnamed x9, local copies, waits for them, and re-layouts  1.28 us

profile of v5, /device:TPU:1, one launch (start us, length us, event | category | flops | bytes accessed | tf_op | source)
XLA Modules:
  0.0 49.0 jit_solution(3167137601495719043)
XLA Ops:
  1.3 0.0 copy-start.1
  1.3 0.0 copy-start.3
  1.3 0.0 copy-start
  1.3 0.0 copy-start.2
  1.3 0.6 %copy-done.1 = f32[1,16,2]{1,2,0:T(2,128)S(1)} copy-done((f32[1,16,2]{1,2,0:T(2,128)S(1)}, f32[1,16,2]{1,2,0:T(2,128)}, u32[]{:S(2)}) %copy-start.1) | copy-done | bytes 152
  2.0 0.0 copy-done.3
  2.0 0.0 copy-done
  2.0 0.0 copy-done.2
  2.0 46.4 %shard_map.82 = f32[1,2,2,192]{3,2,1,0:T(2,128)S(1)} custom-call(bf16[1,2,16,16384]{3,2,1,0:T(8,128)(2,1)} %rec.1, bf16[1,2,192,256]{3,2,1,0:T(8,128)(2,1)} %mir.1, s32[1,1]{1,0:T(1,128)S(6)} %copy.10.live_hbm, s32[2,16]{1,0:T(2,128)S(1)} %bitcast.8, f32[2,16]{1,0:T(2,128)S(1)} %bitcast.9, s32[1,16]{1,0:T(1,128)S(1)} %copy-done.2, s32[1,16]{1,0:T(1,128)S(1)} %copy-done.3, ...), custom_call_target="tpu_custom_call" | custom-call | tf_op jit(solution)/shard_map/pallas_call | solution.py:326
  48.4 0.6 %copy.12 = f32[1,2,2,192]{3,2,1,0:T(2,128)} copy(f32[1,2,2,192]{3,2,1,0:T(2,128)S(1)} %shard_map.82) | data formatting | bytes 6144
Async XLA Ops:
  1.3 0.7 %copy-start.1 = (f32[1,16,2]{1,2,0:T(2,128)S(1)}, f32[1,16,2]{1,2,0:T(2,128)}, u32[]{:S(2)}) copy-start(f32[1,16,2]{1,2,0:T(2,128)} %param.12) | copy-start | bytes 388
  1.3 0.7 %copy-start.3 = (s32[1,16]{1,0:T(1,128)S(1)}, s32[1,16]{1,0:T(1,128)}, u32[]{:S(2)}) copy-start(s32[1,16]{1,0:T(1,128)} %hi_hbm.1) | copy-start | bytes 196
  1.3 0.7 %copy-start = (s32[1,16,2]{1,2,0:T(2,128)S(1)}, s32[1,16,2]{1,2,0:T(2,128)}, u32[]{:S(2)}) copy-start(s32[1,16,2]{1,2,0:T(2,128)} %param.11) | copy-start | bytes 388
  1.3 0.7 %copy-start.2 = (s32[1,16]{1,0:T(1,128)S(1)}, s32[1,16]{1,0:T(1,128)}, u32[]{:S(2)}) copy-start(s32[1,16]{1,0:T(1,128)} %lo_hbm.1) | copy-start | bytes 196

commit v6 on v5

--- a/solution.py
+++ b/solution.py
@@ -25,9 +25,8 @@
     half = NY // 2
     tail = src - 128
 
-    def kernel(rec, mir, live_hbm, bins_hbm, wts_hbm, lo_hbm, hi_hbm, gain_hbm, out,
-               live, bins, wts, lo, hi, gain, raw, sbuf, rraw, rsend, rbuf, meta, mapt, tap, acc, asend, abuf, bsend, bbuf, esend, ebuf,
-               l_sem, p_sem, q_sem, word_p, word_f, s_send, s_recv, r_send, r_recv, m_send, m_recv,
+    def kernel(rec, mir, live, bins, wts, lo, hi, gain, out, raw, sbuf, rraw, rsend, rbuf, meta, mapt, tap, acc, asend, abuf, bsend, bbuf, esend, ebuf,
+               l_sem, q_sem, word_p, word_f, s_send, s_recv, r_send, r_recv, m_send, m_recv,
                a_send, a_recv, b_send, b_recv, e_send, e_recv):
         blk = lax.axis_index("blk")
         frq = lax.axis_index("freq")
@@ -68,15 +67,11 @@
             pl.semaphore_signal(barrier, inc=1, device_id=to, device_id_type=MESH)
 
         loads = [pltpu.make_async_copy(mir.at[0, c], raw.at[c], l_sem.at[c]) for c in range(2)]
-        small = [(live_hbm, live), (bins_hbm, bins), (wts_hbm, wts), (lo_hbm, lo), (hi_hbm, hi), (gain_hbm, gain)]
-        small = [pltpu.make_async_copy(a, b, p_sem.at[i]) for i, (a, b) in enumerate(small)]
-        small[0].start()
         rows_in = pltpu.make_async_copy(rec.at[0], rraw, q_sem)
-        for copy in loads + [rows_in] + small[1:]:
+        for copy in loads + [rows_in]:
             copy.start()
 
-        small[0].wait()
-        on = lax.broadcasted_iota(jnp.int32, (src, k_dev), 1) < live[...]
+        on = lax.broadcasted_iota(jnp.int32, (src, k_dev), 1) < live[0, 0]
         for c in range(2):
             loads[c].wait()
             sbuf[y, c] = jnp.where(on, raw[c], jnp.zeros_like(raw[c]))
@@ -143,9 +138,6 @@
                     meta_copy(i).start()
                     rows_copy(i).start()
 
-
-        for copy in small[1:]:
-            copy.wait()
 
         def column(line):
             line = jnp.broadcast_to(line.astype(F32), (r_dev, r_dev))
@@ -275,7 +267,7 @@
         for d in range(1, NY):
             b_copy(d).wait_recv()
             tile = tile + bbuf[d - 1]
-        scaled = tile * gain[...]
+        scaled = tile * gain[0]
         square = scaled * scaled
         esend[...] = square
 
@@ -320,21 +312,15 @@
         src, k_dev = mirror.shape[2], mirror.shape[3]
         n_plane = NX * NZ
         rows, per, n_peer, half = n_plane * r_dev, 2 * NY, n_plane - 1, NY // 2
-        hbm, vmem = (pl.BlockSpec(memory_space=m) for m in (pltpu.HBM, pltpu.VMEM))
+        hbm, vmem, smem = (pl.BlockSpec(memory_space=m) for m in (pltpu.HBM, pltpu.VMEM, pltpu.SMEM))
         dma = pltpu.SemaphoreType.DMA
         bf16 = jnp.bfloat16
         return pl.pallas_call(
             make_kernel(n_freq, r_dev, src, k_dev),
             out_shape=jax.ShapeDtypeStruct((1, 2, 2, src), F32),
-            in_specs=[hbm] * 8,
+            in_specs=[hbm, hbm, smem, vmem, vmem, vmem, vmem, smem],
             out_specs=vmem,
             scratch_shapes=[
-                pltpu.VMEM((1, 1), jnp.int32),
-                pltpu.VMEM((2, r_dev), jnp.int32),
-                pltpu.VMEM((2, r_dev), F32),
-                pltpu.VMEM((1, r_dev), jnp.int32),
-                pltpu.VMEM((1, r_dev), jnp.int32),
-                pltpu.VMEM((1, 1), F32),
                 pltpu.VMEM((2, src, k_dev), bf16),
                 pltpu.VMEM((NY, 2, src, k_dev), bf16),
                 pltpu.VMEM((2, r_dev, NY * n_plane * k_dev), bf16),
@@ -350,7 +336,7 @@
                 pltpu.VMEM((NY - 1, 8, 128), F32),
                 pltpu.VMEM((8, 128), F32),
                 pltpu.VMEM((n_freq - 1, 8, 128), F32),
-                dma((2,)), dma((6,)), dma, pltpu.SemaphoreType.REGULAR((2,)), pltpu.SemaphoreType.REGULAR((4,)),
+                dma((2,)), dma, pltpu.SemaphoreType.REGULAR((2,)), pltpu.SemaphoreType.REGULAR((4,)),
                 dma((2, 2 * CUTS * half)), dma((2, 2 * CUTS * half)),
                 dma((n_peer,)), dma((n_peer,)),
                 dma((n_peer,)), dma((n_peer,)),
@@ -361,7 +347,7 @@
             compiler_params=pltpu.CompilerParams(
                 collective_id=0, has_side_effects=True, vmem_limit_bytes=55150 * 1024
             ),
-        )(recorded, mirror, live_counts, bins[0].T, bin_weight[0].T, taper_lo, taper_hi, gain.reshape(1, 1))
+        )(recorded, mirror, live_counts, bins[0].T, bin_weight[0].T, taper_lo, taper_hi, gain)
 
     in_specs = (
         P("freq", None, "blk", None),

time: 49.2 us -> 49.1 us (level)
  no operation moved by 1% of the time
where the time goes in v6:
time: 49.1 us; the launch traced here: 48.9 us
  Pallas kernels  46.3 us (94%)
  between operations  1.34 us (3%)
  local copies, waits for them, and re-layouts  1.28 us (3%)
    pallas_call x1, Pallas kernels, local(): pl.pallas_call(make_kernel(n_freq, r_dev, src, k_dev), out_shape=jax.Shap...  46.3 us
    unnamed x9, local copies, waits for them, and re-layouts  1.28 us

profile of v6, /device:TPU:1, one launch (start us, length us, event | category | flops | bytes accessed | tf_op | source)
XLA Modules:
  0.0 48.9 jit_solution(14452850401242009736)
XLA Ops:
  1.3 0.0 copy-start.1
  1.3 0.0 copy-start.3
  1.3 0.0 copy-start
  1.3 0.0 copy-start.2
  1.3 0.6 %copy-done.1 = f32[1,16,2]{1,2,0:T(2,128)S(1)} copy-done((f32[1,16,2]{1,2,0:T(2,128)S(1)}, f32[1,16,2]{1,2,0:T(2,128)}, u32[]{:S(2)}) %copy-start.1) | copy-done | bytes 152
  2.0 0.0 copy-done.3
  2.0 0.0 copy-done
  2.0 0.0 copy-done.2
  2.0 46.3 %shard_map.82 = f32[1,2,2,192]{3,2,1,0:T(2,128)S(1)} custom-call(bf16[1,2,16,16384]{3,2,1,0:T(8,128)(2,1)} %rec.1, bf16[1,2,192,256]{3,2,1,0:T(8,128)(2,1)} %mir.1, s32[1,1]{1,0:T(1,128)S(6)} %copy.10.live, s32[2,16]{1,0:T(2,128)S(1)} %bitcast.6, f32[2,16]{1,0:T(2,128)S(1)} %bitcast.7, s32[1,16]{1,0:T(1,128)S(1)} %copy-done.2, s32[1,16]{1,0:T(1,128)S(1)} %copy-done.3, ...), custom_call_target="tpu_custom_call" | custom-call | tf_op jit(solution)/shard_map/pallas_call | solution.py:318
  48.3 0.6 %copy.12 = f32[1,2,2,192]{3,2,1,0:T(2,128)} copy(f32[1,2,2,192]{3,2,1,0:T(2,128)S(1)} %shard_map.82) | data formatting | bytes 6144
Async XLA Ops:
  1.3 0.7 %copy-start.1 = (f32[1,16,2]{1,2,0:T(2,128)S(1)}, f32[1,16,2]{1,2,0:T(2,128)}, u32[]{:S(2)}) copy-start(f32[1,16,2]{1,2,0:T(2,128)} %param.12) | copy-start | bytes 388
  1.3 0.7 %copy-start.3 = (s32[1,16]{1,0:T(1,128)S(1)}, s32[1,16]{1,0:T(1,128)}, u32[]{:S(2)}) copy-start(s32[1,16]{1,0:T(1,128)} %hi.1) | copy-start | bytes 196
  1.3 0.7 %copy-start = (s32[1,16,2]{1,2,0:T(2,128)S(1)}, s32[1,16,2]{1,2,0:T(2,128)}, u32[]{:S(2)}) copy-start(s32[1,16,2]{1,2,0:T(2,128)} %param.11) | copy-start | bytes 388
  1.3 0.7 %copy-start.2 = (s32[1,16]{1,0:T(1,128)S(1)}, s32[1,16]{1,0:T(1,128)}, u32[]{:S(2)}) copy-start(s32[1,16]{1,0:T(1,128)} %lo.1) | copy-start | bytes 196

commit v7 on v6

--- a/solution.py
+++ b/solution.py
@@ -6,7 +6,7 @@
 from jax.sharding import PartitionSpec as P
 
 RAMP = 24
-CUTS = 1
+CUTS = 2
 NY, NX, NZ, NC = 8, 4, 2, 2
 MESH = pl.DeviceIdType.MESH
 F32 = jnp.float32

time: 49.1 us -> 49.1 us (level)
  no operation moved by 1% of the time
where the time goes in v7:
time: 49.1 us; the launch traced here: 49 us
  Pallas kernels  46.4 us (95%)
  between operations  1.34 us (3%)
  local copies, waits for them, and re-layouts  1.28 us (3%)
    pallas_call x1, Pallas kernels, local(): pl.pallas_call(make_kernel(n_freq, r_dev, src, k_dev), out_shape=jax.Shap...  46.4 us
    unnamed x9, local copies, waits for them, and re-layouts  1.28 us

profile of v7, /device:TPU:1, one launch (start us, length us, event | category | flops | bytes accessed | tf_op | source)
XLA Modules:
  0.0 49.0 jit_solution(16798758694160715126)
XLA Ops:
  1.3 0.0 copy-start.1
  1.3 0.0 copy-start.3
  1.3 0.0 copy-start
  1.3 0.0 copy-start.2
  1.3 0.6 %copy-done.1 = f32[1,16,2]{1,2,0:T(2,128)S(1)} copy-done((f32[1,16,2]{1,2,0:T(2,128)S(1)}, f32[1,16,2]{1,2,0:T(2,128)}, u32[]{:S(2)}) %copy-start.1) | copy-done | bytes 152
  2.0 0.0 copy-done.3
  2.0 0.0 copy-done
  2.0 0.0 copy-done.2
  2.0 46.4 %shard_map.82 = f32[1,2,2,192]{3,2,1,0:T(2,128)S(1)} custom-call(bf16[1,2,16,16384]{3,2,1,0:T(8,128)(2,1)} %rec.1, bf16[1,2,192,256]{3,2,1,0:T(8,128)(2,1)} %mir.1, s32[1,1]{1,0:T(1,128)S(6)} %copy.10.live, s32[2,16]{1,0:T(2,128)S(1)} %bitcast.6, f32[2,16]{1,0:T(2,128)S(1)} %bitcast.7, s32[1,16]{1,0:T(1,128)S(1)} %copy-done.2, s32[1,16]{1,0:T(1,128)S(1)} %copy-done.3, ...), custom_call_target="tpu_custom_call" | custom-call | tf_op jit(solution)/shard_map/pallas_call | solution.py:318
  48.4 0.6 %copy.12 = f32[1,2,2,192]{3,2,1,0:T(2,128)} copy(f32[1,2,2,192]{3,2,1,0:T(2,128)S(1)} %shard_map.82) | data formatting | bytes 6144
Async XLA Ops:
  1.3 0.7 %copy-start.1 = (f32[1,16,2]{1,2,0:T(2,128)S(1)}, f32[1,16,2]{1,2,0:T(2,128)}, u32[]{:S(2)}) copy-start(f32[1,16,2]{1,2,0:T(2,128)} %param.12) | copy-start | bytes 388
  1.3 0.7 %copy-start.3 = (s32[1,16]{1,0:T(1,128)S(1)}, s32[1,16]{1,0:T(1,128)}, u32[]{:S(2)}) copy-start(s32[1,16]{1,0:T(1,128)} %hi.1) | copy-start | bytes 196
  1.3 0.7 %copy-start = (s32[1,16,2]{1,2,0:T(2,128)S(1)}, s32[1,16,2]{1,2,0:T(2,128)}, u32[]{:S(2)}) copy-start(s32[1,16,2]{1,2,0:T(2,128)} %param.11) | copy-start | bytes 388
  1.3 0.7 %copy-start.2 = (s32[1,16]{1,0:T(1,128)S(1)}, s32[1,16]{1,0:T(1,128)}, u32[]{:S(2)}) copy-start(s32[1,16]{1,0:T(1,128)} %lo.1) | copy-start | bytes 196
